TPU v7x, 32 devices: a whole 2x2x4 slice. The times are simulated.
32 devices in a mesh: freq: 16 (over z, x, core), rec: 2 (over y).
Axes of the slice: x: 2, y: 2, z: 4, core: 2. Of those that a mesh axis runs over, the one named last changes fastest.
Arguments:
- kernel: bfloat16 [2, 64, 256, 9216], P(None, 'freq', None, 'rec'), may hold values from -0.09375 to 0.09375
- focusing_in: bfloat16 [32, 9216, 1024], P('freq', 'rec'), may hold values from -6 to 6
- onset_src: int32 [32, 256], P('freq'), may hold values from 128 to 895
- onset_rec: int32 [32, 9216], P('freq', 'rec'), may hold values from 128 to 895
Outputs:
- focusing: bfloat16 [32, 9216, 1024], P('freq', 'rec')
- upgoing_field: bfloat16 [32, 256, 1024], P('freq', 'rec')
All inputs are finite; a program needn't handle non-finite values.
Results may differ from a plain program's by a relative error of at most 0.018.
Values may be sent and summed in bfloat16 or wider, within the bound.
A program may use at most 128 MiB of HBM per device.

v0:
```python
import jax
import jax.numpy as jnp
from jax import lax
from jax.sharding import PartitionSpec as P

LOW = 8
ITERS = 2


def make_tables(count, samples, lowest):
    freqs = (lax.iota(jnp.int32, count) + lowest)[:, None]
    times = lax.iota(jnp.int32, samples)[None, :]
    phase = (freqs * times % samples).astype(jnp.float32) * (2.0 * 3.141592653589793 / samples)
    both = jnp.stack([jnp.cos(phase), -jnp.sin(phase)])
    forward = both.astype(jnp.bfloat16)
    inverse = (forward.astype(jnp.float32) * (2.0 / samples)).astype(jnp.bfloat16)
    return (forward, inverse)


def forward_mdc(block_slice, spread_layout):
    real = jnp.einsum(
        "wch,wah->cwa", block_slice[0], spread_layout[0], preferred_element_type=jnp.float32
    ) - jnp.einsum(
        "wch,wah->cwa", block_slice[1], spread_layout[1], preferred_element_type=jnp.float32
    )
    imag = jnp.einsum(
        "wch,wah->cwa", block_slice[0], spread_layout[1], preferred_element_type=jnp.float32
    ) + jnp.einsum(
        "wch,wah->cwa", block_slice[1], spread_layout[0], preferred_element_type=jnp.float32
    )
    return jnp.stack([real, imag], axis=1)


def adjoint_mdc(block_slice, piece_portion):
    real = jnp.einsum(
        "thl,htv->tvl", block_slice[0], piece_portion[:, 0], preferred_element_type=jnp.float32
    ) + jnp.einsum(
        "thl,htv->tvl", block_slice[1], piece_portion[:, 1], preferred_element_type=jnp.float32
    )
    imag = jnp.einsum(
        "thl,htv->tvl", block_slice[0], piece_portion[:, 1], preferred_element_type=jnp.float32
    ) - jnp.einsum(
        "thl,htv->tvl", block_slice[1], piece_portion[:, 0], preferred_element_type=jnp.float32
    )
    return jnp.stack([real, imag])


def body(kernel, focusing_in, onset_src, onset_rec):
    freq_count = lax.axis_size("freq")
    rec_count = lax.axis_size("rec")
    band = kernel.shape[1] * freq_count
    samples = focusing_in.shape[2]
    sources = kernel.shape[2]
    share = sources // rec_count
    forward, inverse = make_tables(band, samples, LOW)
    times = lax.iota(jnp.int32, samples)
    keep_rec = times[None, None, :] < onset_rec[:, :, None]
    first = lax.axis_index("rec") * share
    focusing = focusing_in
    upgoing_field = None
    for step in range(ITERS):
        spectrum = jnp.einsum(
            "prt,ckt->ckpr", focusing, forward, preferred_element_type=jnp.float32
        ).astype(jnp.bfloat16)
        spread_layout = lax.all_to_all(spectrum, "freq", split_axis=1, concat_axis=2, tiled=True)
        own_onsets = lax.dynamic_slice_in_dim(onset_src, first, share, 1)
        keep_src = times[None, None, :] < own_onsets[:, :, None]
        local = lax.psum_scatter(
            forward_mdc(kernel, spread_layout).astype(jnp.bfloat16),
            "rec",
            scatter_dimension=0,
            tiled=True,
        )
        series = lax.all_to_all(local, "freq", split_axis=3, concat_axis=2, tiled=True)
        signal = jnp.einsum("sckp,ckt->pst", series, inverse, preferred_element_type=jnp.float32)
        upgoing_field = signal.astype(jnp.bfloat16)
        muted = jnp.where(keep_src, signal, 0.0).astype(jnp.bfloat16)
        echo = jnp.einsum(
            "pst,ckt->sckp", muted, forward, preferred_element_type=jnp.float32
        ).astype(jnp.bfloat16)
        returned_output = lax.all_to_all(echo, "freq", split_axis=2, concat_axis=3, tiled=True)
        reflected = adjoint_mdc(kernel, lax.all_gather(returned_output, "rec", axis=0, tiled=True))
        reflected = reflected.astype(jnp.bfloat16)
        arrived = lax.all_to_all(reflected, "freq", split_axis=2, concat_axis=1, tiled=True)
        update = jnp.einsum("ckpr,ckt->prt", arrived, inverse, preferred_element_type=jnp.float32)
        focusing = (focusing_in.astype(jnp.float32) + jnp.where(keep_rec, update, 0.0)).astype(
            jnp.bfloat16
        )
    return (focusing, upgoing_field)


def solution(mesh):
    placed = (
        P(None, "freq", None, "rec"),
        P("freq", "rec", None),
        P("freq", None),
        P("freq", "rec"),
    )
    return jax.shard_map(
        body,
        mesh=mesh,
        in_specs=placed,
        out_specs=(P("freq", "rec", None), P("freq", "rec", None)),
        check_vma=False,
    )
```

profile of v0, /device:TPU:11, one launch (start us, length us, event | category | flops | bytes accessed | tf_op | source)
XLA Modules:
  0.0 487.6 jit_solution(11279037844828426101)
XLA Ops:
  8.5 10.4 %fusion.46 = bf16[2,64,2,4608]{3,1,2,0:T(8,128)(2,1)S(1)} fusion(bf16[2,4608,1024]{2,1,0:T(8,128)(2,1)} %param.5, bf16[1,64,1024]{2,1,0:T(8,128)(2,1)S(1)} %get-tuple-element.13, bf16[1,64,1024]{2,1,0:T(8,128)(2,1)S(1)} %get-tuple-element.12), kind=kOutput, calls=%fused_computation.47 | convolution fusion | flops 2417623040 | bytes 21495808 | tf_op jit(solution)/shard_map/prt,ckt->ckpr/dot_general | solution.py:62
  21.3 59.5 %all_to_all.138 = bf16[2,64,2,4608]{3,2,0,1:T(2,128)(2,1)S(1)} all-to-all(bf16[2,64,2,4608]{3,2,0,1:T(2,128)(2,1)S(1)} %copy.30), channel_id=1, replica_groups=mesh['freq'=16,'rec'=2] {'freq'}, dimensions={1} | all-to-all | bytes 4718592 | tf_op jit(solution)/shard_map/all_to_all | solution.py:65
  88.9 7.0 %fusion.25 = f32[4,32,256]{2,1,0:T(8,128)S(1)} fusion(bf16[4,32,4608]{2,1,0:T(8,128)(2,1)} %squeeze.22, bf16[2,4,256,4608]{3,2,1,0:T(8,128)(2,1)} %param.4), kind=kOutput, calls=%fused_computation.28 | convolution fusion | flops 301989888 | bytes 10747904 | tf_op jit(solution)/shard_map/wch,wah->cwa/dot_general | solution.py:23
  95.9 6.6 %fusion.23 = f32[4,32,256]{2,1,0:T(8,128)S(1)} fusion(bf16[4,32,4608]{2,1,0:T(8,128)(2,1)S(1)} %copy-done.3, bf16[2,4,256,4608]{3,2,1,0:T(8,128)(2,1)} %param.4), kind=kOutput, calls=%fused_computation.26 | convolution fusion | flops 301989888 | bytes 10747904 | tf_op jit(solution)/shard_map/wch,wah->cwa/dot_general | solution.py:28
  102.6 6.7 %fusion.132 = bf16[256,1,4,32]{0,3,2,1:T(8,128)(2,1)S(1)} fusion(f32[4,32,256]{2,1,0:T(8,128)S(1)} %fusion.25, bf16[4,32,4608]{2,1,0:T(8,128)(2,1)S(1)} %copy-done.3, bf16[2,4,256,4608]{3,2,1,0:T(8,128)(2,1)} %param.4), kind=kOutput, calls=%fused_computation.99 | convolution fusion | flops 302055424 | bytes 10813440 | tf_op jit(solution)/shard_map/wch,wah->cwa/dot_general | solution.py:21
  113.0 10.0 %reduce-scatter.7.cloned.1.call-done = bf16[128,256]{1,0:T(8,128)(2,1)} async-done(((bf16[256,256]{1,0:T(8,128)(2,1)}), bf16[128,256]{1,0:T(8,128)(2,1)}) %reduce-scatter.7.cloned.1.call-update) | async-done | bytes 65552
  124.6 6.4 %all-to-all-start.1 = ((bf16[128,2,4,32]{0,2,1,3:T(4,128)(2,1)}), bf16[128,2,4,32]{0,2,1,3:T(4,128)(2,1)S(1)}, u32[]{:S(2)}, u32[]{:S(2)}) async-start(bf16[128,2,4,32]{0,2,1,3:T(4,128)(2,1)} %copy.32), calls=%async_computation.1 | async-start | bytes 131072 | tf_op jit(solution)/shard_map/all_to_all | solution.py:74
  136.0 9.5 %all_to_all.139 = bf16[128,2,64,2]{0,3,1,2:T(2,128)(2,1)S(1)} all-to-all(bf16[128,2,64,2]{0,3,1,2:T(2,128)(2,1)S(1)} %copy.36), channel_id=1, replica_groups=mesh['freq'=16,'rec'=2] {'freq'}, dimensions={2} | all-to-all | bytes 131072 | tf_op jit(solution)/shard_map/all_to_all | solution.py:81
  155.1 5.6 %fusion.21 = f32[4,32,4608]{2,1,0:T(8,128)S(1)} fusion(bf16[2,4,256,4608]{3,2,1,0:T(8,128)(2,1)} %param.4, bf16[256,2,4,32]{0,3,2,1:T(8,128)(2,1)S(1)} %all_gather.6), kind=kOutput, calls=%fused_computation.24 | convolution fusion | flops 301989888 | bytes 11862016 | tf_op jit(solution)/shard_map/thl,htv->tvl/dot_general | solution.py:37
  160.7 5.6 %fusion.76 = bf16[1,4,32,4608]{3,2,1,0:T(8,128)(2,1)S(1)} fusion(f32[4,32,4608]{2,1,0:T(8,128)S(1)} %fusion.19, bf16[2,4,256,4608]{3,2,1,0:T(8,128)(2,1)} %param.4, bf16[256,2,4,32]{0,3,2,1:T(8,128)(2,1)S(1)} %all_gather.6), kind=kOutput, calls=%fused_computation.57 | convolution fusion | flops 303169536 | bytes 13041664 | tf_op jit(solution)/shard_map/thl,htv->tvl/dot_general | solution.py:40
  170.1 59.8 %all_to_all.140 = bf16[2,4,32,4608]{3,1,0,2:T(4,128)(2,1)S(1)} all-to-all(bf16[2,4,32,4608]{3,1,0,2:T(4,128)(2,1)S(1)} %copy.38), channel_id=1, replica_groups=mesh['freq'=16,'rec'=2] {'freq'}, dimensions={2} | all-to-all | bytes 4718592 | tf_op jit(solution)/shard_map/all_to_all | solution.py:84
  231.7 16.7 %fusion.43 = bf16[2,64,2,4608]{3,1,2,0:T(8,128)(2,1)} fusion(bf16[2,4608,1024]{2,1,0:T(8,128)(2,1)} %param.5, s32[2,4608]{1,0:T(2,128)S(1)} %copy-done.10, bf16[2,64,2,4608]{3,2,1,0:T(2,128)(2,1)S(1)} %bitcast.266, bf16[1,64,1024]{2,1,0:T(8,128)(2,1)S(1)} %get-tuple-element.13, bf16[1,64,1024]{2,1,0:T(8,128)(2,1)S(1)} %get-tuple-element.12), kind=kOutput, calls=%fused_computation.46 | convolution fusion | flops 4881252352 | bytes 23891968 | tf_op jit(solution)/shard_map/prt,ckt->ckpr/dot_general | solution.py:62
  252.5 57.8 %all_to_all.141 = bf16[2,64,2,4608]{3,2,0,1:T(2,128)(2,1)S(1)} all-to-all(bf16[2,64,2,4608]{3,2,0,1:T(2,128)(2,1)S(1)} %copy.41), channel_id=1, replica_groups=mesh['freq'=16,'rec'=2] {'freq'}, dimensions={1} | all-to-all | bytes 4718592 | tf_op jit(solution)/shard_map/all_to_all | solution.py:65
  314.1 7.2 %fusion.17 = f32[4,32,256]{2,1,0:T(8,128)} fusion(bf16[4,32,4608]{2,1,0:T(8,128)(2,1)S(1)} %squeeze.27, bf16[2,4,256,4608]{3,2,1,0:T(8,128)(2,1)} %param.4), kind=kOutput, calls=%fused_computation.20 | convolution fusion | flops 301989888 | bytes 10747904 | tf_op jit(solution)/shard_map/wch,wah->cwa/dot_general | solution.py:23
  321.8 6.5 %fusion.15 = f32[4,32,256]{2,1,0:T(8,128)S(1)} fusion(bf16[4,32,4608]{2,1,0:T(8,128)(2,1)S(1)} %squeeze.26, bf16[2,4,256,4608]{3,2,1,0:T(8,128)(2,1)} %param.4), kind=kOutput, calls=%fused_computation.18 | convolution fusion | flops 301989888 | bytes 10747904 | tf_op jit(solution)/shard_map/wch,wah->cwa/dot_general | solution.py:28
  328.3 6.5 %fusion.138 = bf16[256,1,4,32]{0,3,2,1:T(8,128)(2,1)S(1)} fusion(f32[4,32,256]{2,1,0:T(8,128)S(1)} %copy-done.12, bf16[4,32,4608]{2,1,0:T(8,128)(2,1)S(1)} %squeeze.26, bf16[2,4,256,4608]{3,2,1,0:T(8,128)(2,1)} %param.4), kind=kOutput, calls=%fused_computation.101 | convolution fusion | flops 302055424 | bytes 10813440 | tf_op jit(solution)/shard_map/wch,wah->cwa/dot_general | solution.py:21
  334.9 6.6 %fusion.141 = bf16[256,1,4,32]{0,3,2,1:T(8,128)(2,1)S(1)} fusion(f32[4,32,256]{2,1,0:T(8,128)S(1)} %fusion.15, bf16[4,32,4608]{2,1,0:T(8,128)(2,1)S(1)} %squeeze.27, bf16[2,4,256,4608]{3,2,1,0:T(8,128)(2,1)} %param.4), kind=kOutput, calls=%fused_computation.102 | convolution fusion | flops 302055424 | bytes 10813440 | tf_op jit(solution)/shard_map/wch,wah->cwa/dot_general | solution.py:26
  342.2 9.1 %reduce-scatter.9.cloned.1.call-done = bf16[128,256]{1,0:T(8,128)(2,1)} async-done(((bf16[256,256]{1,0:T(8,128)(2,1)}), bf16[128,256]{1,0:T(8,128)(2,1)}) %reduce-scatter.9.cloned.1.call-update) | async-done | bytes 65552
  352.3 10.5 %all_to_all.142 = bf16[128,2,4,32]{0,2,1,3:T(4,128)(2,1)S(1)} all-to-all(bf16[128,2,4,32]{0,2,1,3:T(4,128)(2,1)S(1)} %copy.43), channel_id=1, replica_groups=mesh['freq'=16,'rec'=2] {'freq'}, dimensions={3} | all-to-all | bytes 131072 | tf_op jit(solution)/shard_map/all_to_all | solution.py:74
  363.5 9.5 %all_to_all.143 = bf16[128,2,64,2]{0,3,1,2:T(2,128)(2,1)S(1)} all-to-all(bf16[128,2,64,2]{0,3,1,2:T(2,128)(2,1)S(1)} %copy.46), channel_id=1, replica_groups=mesh['freq'=16,'rec'=2] {'freq'}, dimensions={2} | all-to-all | bytes 131072 | tf_op jit(solution)/shard_map/all_to_all | solution.py:81
  388.1 5.6 %fusion.82 = bf16[1,4,32,4608]{3,2,1,0:T(8,128)(2,1)S(1)} fusion(f32[4,32,4608]{2,1,0:T(8,128)S(1)} %fusion.11, bf16[2,4,256,4608]{3,2,1,0:T(8,128)(2,1)} %param.4, bf16[256,2,4,32]{0,3,2,1:T(8,128)(2,1)S(1)} %all_gather.7), kind=kOutput, calls=%fused_computation.59 | convolution fusion | flops 303169536 | bytes 13041664 | tf_op jit(solution)/shard_map/thl,htv->tvl/dot_general | solution.py:40
  399.0 7.5 %all-to-all-start.7 = ((bf16[2,4,32,4608]{3,1,0,2:T(4,128)(2,1)}), bf16[2,4,32,4608]{3,1,0,2:T(4,128)(2,1)S(1)}, u32[]{:S(2)}, u32[]{:S(2)}) async-start(bf16[2,4,32,4608]{3,1,0,2:T(4,128)(2,1)} %copy.48), calls=%async_computation.7 | async-start | bytes 4718592 | tf_op jit(solution)/shard_map/all_to_all | solution.py:84
  407.4 52.0 %all-to-all-done.7 = bf16[2,4,32,4608]{3,1,0,2:T(4,128)(2,1)S(1)} async-done(((bf16[2,4,32,4608]{3,1,0,2:T(4,128)(2,1)}), bf16[2,4,32,4608]{3,1,0,2:T(4,128)(2,1)S(1)}, u32[]{:S(2)}, u32[]{:S(2)}) %all-to-all-start.7) | async-done | bytes 2359328 | tf_op jit(solution)/shard_map/all_to_all | solution.py:84
  464.4 16.1 %fusion.1 = bf16[2,4608,1024]{2,1,0:T(8,128)(2,1)} fusion(bf16[2,4608,1024]{2,1,0:T(8,128)(2,1)} %param.5, s32[2,4608]{1,0:T(2,128)S(1)} %copy-done.11, bf16[2,64,2,4608]{3,1,0,2:T(8,128)(2,1)S(1)} %all_to_all.129, bf16[1,64,1024]{2,1,0:T(8,128)(2,1)S(1)} %copy-done.9, bf16[1,64,1024]{2,1,0:T(8,128)(2,1)S(1)} %copy-done.6), kind=kOutput, calls=%fused_computation.3 | convolution fusion | flops 2463629312 | bytes 40407040 | tf_op jit(solution)/shard_map/ckpr,ckt->prt/dot_general | solution.py:85
  (110 shorter events, 74.2 us)
Async XLA Ops:
  7.2 123.9 %copy-start = (s32[2,256]{1,0:T(2,128)S(1)}, s32[2,256]{1,0:T(2,128)}, u32[]{:S(2)}) copy-start(s32[2,256]{1,0:T(2,128)} %param.6) | copy-start | bytes 6148
  7.2 115.8 %reduce-scatter.7.cloned.1.call-start = ((), (), s32[]{:S(2)}) async-start(), calls=%async_computation.10 | async-start | bytes 196608
  8.5 223.2 %copy-start.4 = (bf16[1,64,1024]{2,1,0:T(8,128)(2,1)}, bf16[1,64,1024]{2,1,0:T(8,128)(2,1)S(1)}, u32[]{:S(2)}) copy-start(bf16[1,64,1024]{2,1,0:T(8,128)(2,1)S(1)} %get-tuple-element.12) | copy-start | bytes 393220
  8.5 223.2 %copy-start.7 = (bf16[1,64,1024]{2,1,0:T(8,128)(2,1)}, bf16[1,64,1024]{2,1,0:T(8,128)(2,1)S(1)}, u32[]{:S(2)}) copy-start(bf16[1,64,1024]{2,1,0:T(8,128)(2,1)S(1)} %get-tuple-element.13) | copy-start | bytes 393220
  85.1 24.2 %slice-start = ((s8[18874368]{0:T(1024)(128)(4,1)}), s8[2097152]{0:T(1024)(128)(4,1)S(1)}, s32[]{:S(2)}) async-start(s8[18874368]{0:T(1024)(128)(4,1)} %bitcast.253), calls=%async_computation.12 | async-start | bytes 4194304
  88.9 7.0 %copy-start.3 = (bf16[4,32,4608]{2,1,0:T(8,128)(2,1)S(1)}, bf16[4,32,4608]{2,1,0:T(8,128)(2,1)}, u32[]{:S(2)}) copy-start(bf16[4,32,4608]{2,1,0:T(8,128)(2,1)} %squeeze.20) | copy-start | bytes 3538948
  88.9 20.4 %slice-start.1 = ((s8[18874368]{0:T(1024)(128)(4,1)}), s8[4194304]{0:T(1024)(128)(4,1)S(1)}, s32[]{:S(2)}) async-start(s8[18874368]{0:T(1024)(128)(4,1)} %bitcast.253), calls=%async_computation.13 | async-start | bytes 8388608
  88.9 20.4 %slice-start.2 = ((s8[18874368]{0:T(1024)(128)(4,1)}), s8[4194304]{0:T(1024)(128)(4,1)S(1)}, s32[]{:S(2)}) async-start(s8[18874368]{0:T(1024)(128)(4,1)} %bitcast.253), calls=%async_computation.14 | async-start | bytes 8388608
  95.9 13.4 %slice-start.3 = ((s8[18874368]{0:T(1024)(128)(4,1)}), s8[4194304]{0:T(1024)(128)(4,1)S(1)}, s32[]{:S(2)}) async-start(s8[18874368]{0:T(1024)(128)(4,1)} %bitcast.253), calls=%async_computation.15 | async-start | bytes 8388608
  102.6 6.7 %slice-start.4 = ((s8[18874368]{0:T(1024)(128)(4,1)}), s8[4194304]{0:T(1024)(128)(4,1)S(1)}, s32[]{:S(2)}) async-start(s8[18874368]{0:T(1024)(128)(4,1)} %bitcast.253), calls=%async_computation.16 | async-start | bytes 8388608
  102.6 6.8 %copy-start.2 = (bf16[4,32,4608]{2,1,0:T(8,128)(2,1)S(1)}, bf16[4,32,4608]{2,1,0:T(8,128)(2,1)}, u32[]{:S(2)}) copy-start(bf16[4,32,4608]{2,1,0:T(8,128)(2,1)} %squeeze.22) | copy-start | bytes 3538948
  124.6 10.7 %all-to-all-start.1 = ((bf16[128,2,4,32]{0,2,1,3:T(4,128)(2,1)}), bf16[128,2,4,32]{0,2,1,3:T(4,128)(2,1)S(1)}, u32[]{:S(2)}, u32[]{:S(2)}) async-start(bf16[128,2,4,32]{0,2,1,3:T(4,128)(2,1)} %copy.32), calls=%async_computation.1 | async-start | bytes 131072 | tf_op jit(solution)/shard_map/all_to_all | solution.py:74
  131.1 220.3 %reduce-scatter.9.cloned.1.call-start = ((), (), s32[]{:S(2)}) async-start(), calls=%async_computation.11 | async-start | bytes 196608
  149.6 16.7 %slice-start.5 = ((s8[18874368]{0:T(1024)(128)(4,1)}), s8[4194304]{0:T(1024)(128)(4,1)S(1)}, s32[]{:S(2)}) async-start(s8[18874368]{0:T(1024)(128)(4,1)} %bitcast.255), calls=%async_computation.17 | async-start | bytes 8388608
  149.6 16.7 %slice-start.6 = ((s8[18874368]{0:T(1024)(128)(4,1)}), s8[4194304]{0:T(1024)(128)(4,1)S(1)}, s32[]{:S(2)}) async-start(s8[18874368]{0:T(1024)(128)(4,1)} %bitcast.255), calls=%async_computation.18 | async-start | bytes 8388608
  155.1 11.2 %slice-start.7 = ((s8[18874368]{0:T(1024)(128)(4,1)}), s8[4194304]{0:T(1024)(128)(4,1)S(1)}, s32[]{:S(2)}) async-start(s8[18874368]{0:T(1024)(128)(4,1)} %bitcast.255), calls=%async_computation.19 | async-start | bytes 8388608
  321.7 6.5 %copy-start.12 = (f32[4,32,256]{2,1,0:T(8,128)S(1)}, f32[4,32,256]{2,1,0:T(8,128)}, u32[]{:S(2)}) copy-start(f32[4,32,256]{2,1,0:T(8,128)} %fusion.17) | copy-start | bytes 393220
  334.8 28.0 %copy-start.5 = (bf16[1,64,1024]{2,1,0:T(8,128)(2,1)S(1)}, bf16[1,64,1024]{2,1,0:T(8,128)(2,1)}, u32[]{:S(2)}) copy-start(bf16[1,64,1024]{2,1,0:T(8,128)(2,1)} %copy-done.4) | copy-start | bytes 393220
  334.8 28.0 %copy-start.8 = (bf16[1,64,1024]{2,1,0:T(8,128)(2,1)S(1)}, bf16[1,64,1024]{2,1,0:T(8,128)(2,1)}, u32[]{:S(2)}) copy-start(bf16[1,64,1024]{2,1,0:T(8,128)(2,1)} %copy-done.7) | copy-start | bytes 393220
  377.0 16.7 %slice-start.10 = ((s8[18874368]{0:T(1024)(128)(4,1)}), s8[4194304]{0:T(1024)(128)(4,1)S(1)}, s32[]{:S(2)}) async-start(s8[18874368]{0:T(1024)(128)(4,1)} %bitcast.257), calls=%async_computation.22 | async-start | bytes 8388608
  377.0 16.7 %slice-start.11 = ((s8[18874368]{0:T(1024)(128)(4,1)}), s8[4194304]{0:T(1024)(128)(4,1)S(1)}, s32[]{:S(2)}) async-start(s8[18874368]{0:T(1024)(128)(4,1)} %bitcast.257), calls=%async_computation.23 | async-start | bytes 8388608
  382.6 11.2 %slice-start.12 = ((s8[18874368]{0:T(1024)(128)(4,1)}), s8[4194304]{0:T(1024)(128)(4,1)S(1)}, s32[]{:S(2)}) async-start(s8[18874368]{0:T(1024)(128)(4,1)} %bitcast.257), calls=%async_computation.24 | async-start | bytes 8388608
  399.0 60.5 %all-to-all-start.7 = ((bf16[2,4,32,4608]{3,1,0,2:T(4,128)(2,1)}), bf16[2,4,32,4608]{3,1,0,2:T(4,128)(2,1)S(1)}, u32[]{:S(2)}, u32[]{:S(2)}) async-start(bf16[2,4,32,4608]{3,1,0,2:T(4,128)(2,1)} %copy.48), calls=%async_computation.7 | async-start | bytes 4718592 | tf_op jit(solution)/shard_map/all_to_all | solution.py:84
  464.4 16.1 %copy-start.1 = (s32[2,256]{1,0:T(2,128)S(1)}, s32[2,256]{1,0:T(2,128)}, u32[]{:S(2)}) copy-start(s32[2,256]{1,0:T(2,128)} %param.6) | copy-start | bytes 6148
  (8 other events, 32.5 us)
Sparse Core Ops, SparseCore 0:
  113.1 9.8 reduce-scatter.6
  342.4 8.9 reduce-scatter.8
where the time goes:
time: 493 us; the launch traced here: 488 us
  blocking collectives  215 us (44%)
  matrix products  131 us (27%)
  waiting for transfers between devices  75.4 us (15%)
  local copies, waits for them, and re-layouts  36.1 us (7%)
  between operations  14.9 us (3%)
  starting transfers between devices  13.9 us (3%)
    all_to_all x2, blocking collectives, body(): lax.all_to_all(spectrum, 'freq', split_axis=1, concat_axis=2, tiled=True)  117 us
    all_to_all x1, blocking collectives, body(): lax.all_to_all(reflected, 'freq', split_axis=2, concat_axis=1, tiled=True)  59.8 us
    all_to_all x1, waiting for transfers between devices, body(): lax.all_to_all(reflected, 'freq', split_axis=2, concat_axis=1, tiled=True)  52 us
    dot_general x2, matrix products, body(): jnp.einsum('prt,ckt->ckpr', focusing, forward, preferred_element_type=jnp...  27 us
    unnamed x4, waiting for transfers between devices  19.2 us
    all_to_all x2, blocking collectives, body(): lax.all_to_all(echo, 'freq', split_axis=2, concat_axis=3, tiled=True)  18.9 us
    dot_general x1, matrix products, body(): jnp.einsum('ckpr,ckt->prt', arrived, inverse, preferred_element_type=jnp....  16.1 us
    dot_general x2, matrix products, forward_mdc(): jnp.einsum('wch,wah->cwa', block_slice[1], spread_layout[1], preferred_el...  14.2 us
  transfers between devices with their start and end apart: 4, of which 4 were waited for; matrix products, arithmetic and copies ran while one was open for 0% of the time, Pallas kernels for 0%

commit v1 on v0

v1 whole, which is shorter than its diff:
```python
import functools

import jax
import jax.numpy as jnp
import ml_dtypes
import numpy as np
from jax import lax
from jax.experimental import pallas as pl
from jax.experimental.pallas import tpu as pltpu
from jax.sharding import PartitionSpec as P

LOW = 8
ITERS = 2
MESH = pl.DeviceIdType.MESH
BF16 = jnp.bfloat16
F32 = jnp.float32


def make_tables(count, samples, lowest, points, per):
    freqs = (np.arange(count, dtype=np.int64) + lowest)[:, None]
    times = np.arange(samples, dtype=np.int64)[None, :]
    phase = (freqs * times % samples).astype(np.float32) * np.float32(2.0 * np.pi / samples)
    phase = phase.astype(np.float64)
    both = np.stack([np.cos(phase), -np.sin(phase)]).astype(np.float32).astype(ml_dtypes.bfloat16)
    both = both.astype(np.float32)
    owners = count // per
    rows = both.reshape(2, owners, per, samples).transpose(1, 2, 0, 3)
    full = np.zeros((points, owners, points, per, 2, samples), np.float32)
    for p in range(points):
        full[p, :, p] = rows
    full = full.reshape(points, owners * points * per * 2, samples)
    forward = full.astype(ml_dtypes.bfloat16)
    inverse = (full * np.float32(2.0 / samples)).astype(ml_dtypes.bfloat16)
    return forward, inverse


def pick(length, sizes):
    for size in sizes:
        if length % size == 0:
            return size
    return length


def dot_nt(a, b):
    return lax.dot_general(a, b, (((1,), (1,)), ((), ())), preferred_element_type=F32)


def dot_tn(a, b):
    return lax.dot_general(a, b, (((0,), (0,)), ((), ())), preferred_element_type=F32)


def exchange(me, count, src, dst, ssem, rsem):
    dst[me] = src[me]

    @pl.loop(1, count)
    def _(d):
        peer = lax.rem(me + d, count)
        pltpu.make_async_remote_copy(
            src_ref=src.at[peer],
            dst_ref=dst.at[me],
            send_sem=ssem,
            recv_sem=rsem,
            device_id={"freq": peer},
            device_id_type=MESH,
        ).start()


def settle(count, ref, sem):
    part = ref.at[pl.ds(0, count - 1)]
    pltpu.make_async_copy(part, part, sem).wait()


def mega(
    nf, nr, per, points, chunk, sub,
    kern, fin, ons_rec, ons_src, fwd, inv,
    outq, upgoing,
    kv, send_s, recv_s, send_q, recv_q, finbuf, acc, hmat, gp_send, gp_recv, g_send, g_recv, h_send, h_recv, field,
    ksem, fsem, ss_s, rs_s, ss_q, rs_q, ss_p, rs_p, ss_g, rs_g, ss_h, rs_h, osem,
):
    me = lax.axis_index("freq")
    mr = lax.axis_index("rec")
    chunks, rows, width = kv.shape
    sources = acc.shape[1]
    lanes = acc.shape[2]
    samples = fin.shape[2]
    share = upgoing.shape[1]
    block = lanes // nf
    halves = rows // sources
    times = lax.broadcasted_iota(jnp.int32, (1, samples), 1)

    def kload(ch):
        return pltpu.make_async_copy(
            kern.at[:, pl.ds(pl.multiple_of(ch * chunk, chunk), chunk)], kv.at[ch], ksem.at[ch]
        )

    def fload(ch, slot):
        return pltpu.make_async_copy(
            fin.at[:, pl.ds(pl.multiple_of(ch * chunk, chunk), chunk), :], finbuf.at[slot], fsem.at[slot]
        )

    def prefetch():
        for slot in range(min(2, chunks)):
            fload(slot, slot).start()

    def after(ch, slot):
        @pl.when(ch + 2 < chunks)
        def _():
            fload(ch + 2, slot).start()

    prefetch()
    for ch in range(chunks):
        kload(ch).start()

    barrier = pltpu.get_barrier_semaphore()

    @pl.loop(1, nf)
    def _(d):
        pl.semaphore_signal(barrier, inc=1, device_id={"freq": lax.rem(me + d, nf)}, device_id_type=MESH)

    @pl.loop(1, nr)
    def _(d):
        pl.semaphore_signal(barrier, inc=1, device_id={"rec": lax.rem(mr + d, nr)}, device_id_type=MESH)

    pl.semaphore_wait(barrier, nf - 1 + nr - 1)

    @pl.loop(0, chunks)
    def _(ch):
        slot = lax.rem(ch, 2)
        fload(ch, slot).wait()

        @pl.loop(0, chunk // sub)
        def _(i):
            at = pl.ds(pl.multiple_of(i * sub, sub), sub)
            spec = dot_nt(fwd[0], finbuf[slot, 0, at, :])
            for p in range(1, points):
                spec += dot_nt(fwd[p], finbuf[slot, p, at, :])
            send_s[ch, :, :, at] = spec.astype(BF16).reshape(nf, block, sub)

        after(ch, slot)
        exchange(me, nf, send_s.at[ch], recv_s.at[ch], ss_s.at[ch], rs_s.at[ch])

    for it in range(ITERS):
        last = it == ITERS - 1
        if not last:
            prefetch()
        acc[...] = jnp.zeros_like(acc)

        @pl.loop(0, chunks)
        def _(ch):
            if it == 0:
                kload(ch).wait()
            settle(nf, recv_s.at[ch], rs_s.at[ch])
            settle(nf, send_s.at[ch], ss_s.at[ch])

            @pl.loop(0, halves)
            def _(j):
                at = pl.ds(pl.multiple_of(j * sources, sources), sources)
                acc[j] += dot_nt(kv[ch, at, :], recv_s[ch].reshape(lanes, width))

        lane = lax.broadcasted_iota(jnp.int32, (1, lanes), 1)
        imag = lax.rem(lane, 2) == 1
        which = lax.rem(lax.div(lane, 2), per)
        total = jnp.zeros((sources, lanes), F32)
        for k in range(per):
            one = acc[k]
            two = acc[per + k]
            swapped = jnp.where(imag, pltpu.roll(two, 1, 1), -pltpu.roll(two, lanes - 1, 1))
            total = jnp.where(which == k, one + swapped, total)
        gp_send[it] = total.T.astype(BF16)

        def partial(d, slot):
            return pltpu.make_async_remote_copy(
                src_ref=gp_send.at[it],
                dst_ref=gp_recv.at[it, slot],
                send_sem=ss_p.at[it, d - 1],
                recv_sem=rs_p.at[it, slot],
                device_id={"rec": lax.rem(mr + d, nr)},
                device_id_type=MESH,
            )

        for d in range(1, nr):
            partial(d, d - 1).start()
        full = gp_send[it].astype(F32)
        for d in range(1, nr):
            partial(d, d - 1).wait()
            full += gp_recv[it, d - 1].astype(F32)
        g_send[it] = full.astype(BF16).reshape(nf, block, sources)
        exchange(me, nf, g_send.at[it], g_recv.at[it], ss_g.at[it], rs_g.at[it])
        settle(nf, g_recv.at[it], rs_g.at[it])
        settle(nf, g_send.at[it], ss_g.at[it])

        got = g_recv[it].reshape(lanes, sources)
        echo = jnp.zeros((lanes, sources), F32)
        for p in range(points):
            signal = dot_tn(got, inv[p])
            if last:
                field[p] = signal.astype(BF16)
            muted = jnp.where(times < ons_src[:, p : p + 1], signal, 0.0).astype(BF16)
            echo += dot_nt(fwd[p], muted)
        h_send[it] = echo.astype(BF16).reshape(nf, block, sources)
        exchange(me, nf, h_send.at[it], h_recv.at[it], ss_h.at[it], rs_h.at[it])
        if last:
            mine = pl.ds(pl.multiple_of(mr * share, share), share)
            upgoing[...] = field[:, mine, :]
        settle(nf, h_recv.at[it], rs_h.at[it])
        settle(nf, h_send.at[it], ss_h.at[it])

        straight = h_recv[it].reshape(lanes, sources).astype(F32)
        row = lax.broadcasted_iota(jnp.int32, (lanes, 1), 0)
        imag = lax.rem(row, 2) == 1
        which = lax.rem(lax.div(row, 2), per)
        crossed = jnp.where(imag, -pltpu.roll(straight, 1, 0), pltpu.roll(straight, lanes - 1, 0))
        for c, value in enumerate((straight, crossed)):
            for k in range(per):
                at = (c * per + k) * sources
                hmat[:, at : at + sources] = jnp.where(which == k, value, 0.0).astype(BF16)

        @pl.loop(0, chunks)
        def _(ch):
            back = jnp.dot(hmat[...], kv[ch], preferred_element_type=F32)
            send_q[ch] = back.astype(BF16).reshape(nf, block, width)
            exchange(me, nf, send_q.at[ch], recv_q.at[ch], ss_q.at[ch], rs_q.at[ch])

        @pl.loop(0, chunks)
        def _(ch):
            slot = lax.rem(ch, 2)
            settle(nf, recv_q.at[ch], rs_q.at[ch])
            settle(nf, send_q.at[ch], ss_q.at[ch])
            if last:
                pltpu.make_async_copy(recv_q.at[ch], outq.at[ch], osem.at[ch]).start()
            else:
                fload(ch, slot).wait()

                @pl.loop(0, chunk // sub)
                def _(i):
                    at = pl.ds(pl.multiple_of(i * sub, sub), sub)
                    there = pl.ds(pl.multiple_of(ch * chunk + i * sub, sub), sub)
                    arrived = recv_q[ch, :, :, at].reshape(lanes, sub)
                    spec = jnp.zeros((lanes, sub), F32)
                    for p in range(points):
                        update = dot_tn(arrived, inv[p])
                        kept = jnp.where(times < ons_rec[there, p : p + 1], update, 0.0)
                        focus = (finbuf[slot, p, at, :].astype(F32) + kept).astype(BF16)
                        spec += dot_nt(fwd[p], focus)
                    send_s[ch, :, :, at] = spec.astype(BF16).reshape(nf, block, sub)

                after(ch, slot)
                exchange(me, nf, send_s.at[ch], recv_s.at[ch], ss_s.at[ch], rs_s.at[ch])

    @pl.loop(0, chunks)
    def _(ch):
        pltpu.make_async_copy(recv_q.at[ch], outq.at[ch], osem.at[ch]).wait()


def finish(arrived, fin, ons, inv, out):
    got = arrived[0].reshape(inv.shape[1], arrived.shape[3])
    times = lax.broadcasted_iota(jnp.int32, (1, inv.shape[2]), 1)
    for p in range(out.shape[0]):
        update = dot_tn(got, inv[p])
        kept = jnp.where(times < ons[:, p : p + 1], update, 0.0)
        out[p] = (fin[p].astype(F32) + kept).astype(BF16)


def body(kernel, focusing_in, onset_src, onset_rec):
    nf = lax.axis_size("freq")
    nr = lax.axis_size("rec")
    parts, per, sources, receivers = kernel.shape
    points, _, samples = focusing_in.shape
    share = sources // nr
    chunk = pick(receivers, (768, 384, 256, 128))
    sub = pick(chunk, (256, 128))
    chunks = receivers // chunk
    block = points * per * 2
    lanes = nf * block
    rows = parts * per * sources
    forward, inverse = make_tables(per * nf, samples, LOW, points, per)
    forward, inverse = jnp.asarray(forward), jnp.asarray(inverse)
    ons_rec, ons_src = onset_rec.T, onset_src.T
    vmem = pl.BlockSpec(memory_space=pltpu.VMEM)
    anywhere = pl.BlockSpec(memory_space=pl.ANY)
    big = pltpu.VMEM((chunks, nf, block, chunk), BF16)
    small = pltpu.VMEM((ITERS, nf, block, sources), BF16)
    dma = pltpu.SemaphoreType.DMA
    arrived, upgoing = pl.pallas_call(
        functools.partial(mega, nf, nr, per, points, chunk, sub),
        out_shape=(
            jax.ShapeDtypeStruct((chunks, nf, block, chunk), BF16),
            jax.ShapeDtypeStruct((points, share, samples), BF16),
        ),
        in_specs=[anywhere, anywhere, vmem, vmem, vmem, vmem],
        out_specs=(anywhere, vmem),
        scratch_shapes=[
            pltpu.VMEM((chunks, rows, chunk), BF16),
            big, big, big, big,
            pltpu.VMEM((2, points, chunk, samples), BF16),
            pltpu.VMEM((rows // sources, sources, lanes), F32),
            pltpu.VMEM((lanes, rows), BF16),
            pltpu.VMEM((ITERS, lanes, sources), BF16),
            pltpu.VMEM((ITERS, max(nr - 1, 1), lanes, sources), BF16),
            small, small, small, small,
            pltpu.VMEM((points, sources, samples), BF16),
            dma((chunks,)), dma((2,)),
            dma((chunks,)), dma((chunks,)), dma((chunks,)), dma((chunks,)),
            dma((ITERS, max(nr - 1, 1))), dma((ITERS, max(nr - 1, 1))),
            dma((ITERS,)), dma((ITERS,)), dma((ITERS,)), dma((ITERS,)),
            dma((chunks,)),
        ],
        compiler_params=pltpu.CompilerParams(
            collective_id=0, has_side_effects=True, vmem_limit_bytes=60 * 1024 * 1024
        ),
        name="marchenko",
    )(kernel.reshape(rows, receivers), focusing_in, ons_rec, ons_src, forward, inverse)

    per_chunk = chunk // sub
    focusing = pl.pallas_call(
        finish,
        grid=(receivers // sub,),
        out_shape=jax.ShapeDtypeStruct(focusing_in.shape, BF16),
        in_specs=[
            pl.BlockSpec((1, nf, block, sub), lambda i: (i // per_chunk, 0, 0, i % per_chunk)),
            pl.BlockSpec((points, sub, samples), lambda i: (0, i, 0)),
            pl.BlockSpec((sub, points), lambda i: (i, 0)),
            pl.BlockSpec((points, lanes, samples), lambda i: (0, 0, 0)),
        ],
        out_specs=pl.BlockSpec((points, sub, samples), lambda i: (0, i, 0)),
        compiler_params=pltpu.CompilerParams(vmem_limit_bytes=40 * 1024 * 1024),
        name="finish",
    )(arrived, focusing_in, ons_rec, inverse)
    return (focusing, upgoing)


def solution(mesh):
    placed = (
        P(None, "freq", None, "rec"),
        P("freq", "rec", None),
        P("freq", None),
        P("freq", "rec"),
    )
    return jax.shard_map(
        body,
        mesh=mesh,
        in_specs=placed,
        out_specs=(P("freq", "rec", None), P("freq", "rec", None)),
        check_vma=False,
    )
```

time: 493 us -> 291 us (0.59)
  Pallas kernels: 0 us -> 282 us
  blocking collectives: 215 us -> 0 us
  matrix products: 131 us -> 0 us
  waiting for transfers between devices: 75.4 us -> 0 us
  local copies, waits for them, and re-layouts: 36.1 us -> 6.82 us
  between operations: 14.9 us -> 0.67 us
  starting transfers between devices: 13.9 us -> 0 us
    pallas_call x0 -> x2, Pallas kernels: none -> 282 us  [the longest x1 260 us: body(): pl.pallas_call(functools.partial(mega, nf, nr, per, points, chunk, sub),...]
    all_to_all x6 -> x0, blocking collectives: 207 us -> none  [the longest x2 117 us: body(): lax.all_to_all(spectrum, 'freq', split_axis=1, concat_axis=2, tiled=True)]
    dot_general x22 -> x0, matrix products: 131 us -> none  [the longest x2 27 us: body(): jnp.einsum('prt,ckt->ckpr', focusing, forward, preferred_element_type=jnp...]
    all_to_all x2 -> x0, waiting for transfers between devices: 56.2 us -> none  [the longest x1 52 us: body(): lax.all_to_all(reflected, 'freq', split_axis=2, concat_axis=1, tiled=True)]
    unnamed x4 -> x0, waiting for transfers between devices: 19.2 us -> none
    all_to_all x2 -> x0, starting transfers between devices: 13.9 us -> none  [the longest x1 7.46 us: body(): lax.all_to_all(reflected, 'freq', split_axis=2, concat_axis=1, tiled=True)]
    all_to_all x9 -> x0, local copies, waits for them, and re-layouts: 10.1 us -> none  [the longest x3 6.71 us: body(): lax.all_to_all(reflected, 'freq', split_axis=2, concat_axis=1, tiled=True)]
    all_gather x2 -> x0, blocking collectives: 8.09 us -> none  [body(): lax.all_gather(returned_output, 'rec', axis=0, tiled=True)]
  transfers between devices with their start and end apart: 4 -> 0, of which waited for: 4 -> 0; matrix products, arithmetic and copies ran while one was open for 0% -> 0% of each run, Pallas kernels for 0% -> 0%
where the time goes in v1:
time: 291 us; the launch traced here: 290 us
  Pallas kernels  282 us (97%)
  local copies, waits for them, and re-layouts  6.82 us (2%)
    pallas_call x1, Pallas kernels, body(): pl.pallas_call(functools.partial(mega, nf, nr, per, points, chunk, sub),...  260 us
    pallas_call x1, Pallas kernels, body(): pl.pallas_call(finish, grid=(receivers // sub,), out_shape=jax.ShapeDtype...  22.4 us
    unnamed x11, local copies, waits for them, and re-layouts  6.82 us

profile of v1, /device:TPU:11, one launch (start us, length us, event | category | flops | bytes accessed | tf_op | source)
XLA Modules:
  0.0 289.8 jit_solution(6971567794205714306)
XLA Ops:
  0.6 1.5 copy.9
  2.1 2.9 copy.8
  5.0 0.0 copy-start
  5.0 0.0 copy-start.1
  5.0 260.0 %marchenko.1 = (bf16[6,16,16,768]{3,2,1,0:T(8,128)(2,1)}, bf16[2,128,1024]{2,1,0:T(8,128)(2,1)}) custom-call(bf16[2048,4608]{1,0:T(8,128)(2,1)} %bitcast.5, bf16[2,4608,1024]{2,1,0:T(8,128)(2,1)} %fin.3, s32[4608,2]{1,0:T(8,128)} %bitcast.3, s32[256,2]{1,0:T(8,128)} %bitcast.6, bf16[2,256,1024]{2,1,0:T(8,128)(2,1)} %constant.4.clone.fwd, ...), custom_call_target="tpu_custom_call" | custom-call | tf_op jit(solution)/shard_map/marchenko/pallas_call | solution.py:284
  265.0 0.0 copy-done
  265.0 0.0 copy-done.1
  265.0 0.0 copy-start.2
  265.0 1.7 copy-done.2
  266.7 0.0 copy-start.3
  266.7 22.4 %finish.1 = bf16[2,4608,1024]{2,1,0:T(8,128)(2,1)} custom-call(bf16[6,16,16,768]{3,2,1,0:T(8,128)(2,1)S(1)} %copy-done.2, bf16[2,4608,1024]{2,1,0:T(8,128)(2,1)} %fin.3, s32[4608,2]{1,0:T(8,128)S(1)} %bitcast.4, bf16[2,256,1024]{2,1,0:T(8,128)(2,1)S(1)} %copy-done.1), custom_call_target="tpu_custom_call" | custom-call | tf_op jit(solution)/shard_map/finish/pallas_call | solution.py:315
  289.0 0.0 copy-done.3
  289.0 0.8 copy.11
Async XLA Ops:
  5.0 260.0 %copy-start = (s32[2,4608]{0,1:T(8,128)S(1)}, s32[2,4608]{0,1:T(8,128)}, u32[]{:S(2)}) copy-start(s32[2,4608]{0,1:T(8,128)} %copy.8) | copy-start | bytes 110596
  5.0 260.0 %copy-start.1 = (bf16[2,256,1024]{2,1,0:T(8,128)(2,1)S(1)}, bf16[2,256,1024]{2,1,0:T(8,128)(2,1)}, u32[]{:S(2)}) copy-start(bf16[2,256,1024]{2,1,0:T(8,128)(2,1)} %constant.5.clone.inv) | copy-start | bytes 3145732
  265.0 1.7 copy-start.2
  266.7 22.4 %copy-start.3 = (bf16[2,128,1024]{2,1,0:T(8,128)(2,1)S(1)}, bf16[2,128,1024]{2,1,0:T(8,128)(2,1)}, u32[]{:S(2)}) copy-start(bf16[2,128,1024]{2,1,0:T(8,128)(2,1)} %get-tuple-element.9) | copy-start | bytes 1572868
